TPU v7x, 32 devices: a whole 2x2x4 slice. The times are simulated.
32 devices in a mesh: groups: 2 (over x), seq: 8 (over z, y), head: 2 (over core).
Axes of the slice: x: 2, y: 2, z: 4, core: 2. Of those that a mesh axis runs over, the one named last changes fastest.
Arguments:
- tokens: bfloat16 [8192, 3072], P(('groups', 'seq')), parts along dimension 0, may hold values from -6 to 6
- w_query: bfloat16 [32, 3072, 128], P('head', 'seq'), may hold values from -0.109375 to 0.109375
- w_key: bfloat16 [32, 3072, 128], P('head', 'seq'), may hold values from -0.109375 to 0.109375
- w_value: bfloat16 [32, 3072, 128], P('head', 'seq'), may hold values from -0.109375 to 0.109375
- norm_gain: float32 [32, 128], P('head'), may hold values from 0.25 to 1.75
- log_decay: bfloat16 [32, 8192], P('head', ('groups', 'seq')), parts along dimension 1, may hold values from -1 to 0
- lengths: int32 [8], P('groups'), parts along dimension 0, may hold values from 1 to 2048, 4096 in all
Outputs:
- output: bfloat16 [8192, 32, 128], P(('groups', 'seq'), 'head'), parts along dimension 0
There are 2 independent parts, one for each index of `groups`. A program takes and returns all parts, laid end to end along the dimension named above; an argument that names none is the same for every part. Nothing has to cross between parts.
Inputs may be any that keep to these rules, and one draw needn't show every extreme that they name: The 4 lengths sum to 4096.
All inputs are finite; a program needn't handle non-finite values.
Results may differ from a plain program's by a relative error of at most 0.007.
Values may be sent and summed in bfloat16 or wider, within the bound.
A program may use at most 128 MiB of HBM per device.

v0:
```python
import jax
import jax.numpy as jnp
from jax import lax
from jax.sharding import PartitionSpec as P

BLOCK = 128


def entering(value, axis, join, neutral):
    count, mine = (lax.axis_size(axis), lax.axis_index(axis))
    pieces = jax.tree.map(lambda part: lax.all_gather(part, axis), value)
    total = jax.tree.map(
        lambda part, zero: jnp.full_like(part, 0) + jnp.asarray(zero, part.dtype), value, neutral
    )

    def step(position, total):
        longer = join(total, jax.tree.map(lambda part: part[position], pieces))
        return jax.tree.map(lambda new, old: jnp.where(position < mine, new, old), longer, total)

    return lax.fori_loop(0, count - 1, step, total)


def segment_info(lengths, first_pos, rows_here):
    positions = first_pos + jnp.arange(rows_here, dtype=jnp.int32)
    prompt_ends = jnp.cumsum(lengths)
    prompt_begins = prompt_ends - lengths
    is_start = jnp.any(positions[:, None] == prompt_begins[None, :], axis=1)
    segment = jnp.sum((positions[:, None] >= prompt_ends[None, :]).astype(jnp.int32), axis=1)
    return (is_start, segment)


def local_blocks(query, keys, value_rows, log_decay, is_start, segment, block_len):
    rows_here, heads_here, head_size = query.shape
    blocks = rows_here // block_len
    query_blk = query.reshape(blocks, block_len, heads_here, head_size)
    keys_blk = keys.reshape(blocks, block_len, heads_here, head_size)
    values_blk = value_rows.reshape(blocks, block_len, heads_here, head_size)
    running = jnp.cumsum(
        log_decay.astype(jnp.float32).reshape(heads_here, blocks, block_len), axis=2
    )
    starts_seen = jnp.cumsum(is_start.reshape(blocks, block_len).astype(jnp.int32), axis=1)
    started = starts_seen > 0
    later_start = starts_seen[:, -1:] - starts_seen > 0
    prompt_ids = segment.reshape(blocks, block_len)
    offsets = jnp.arange(block_len)
    visible = (offsets[:, None] >= offsets[None, :])[None] & (
        prompt_ids[:, :, None] == prompt_ids[:, None, :]
    )
    gap_log = running[:, :, :, None] - running[:, :, None, :]
    decay_w = jnp.where(visible[None], jnp.exp(jnp.where(visible[None], gap_log, 0.0)), 0.0)
    scores = jnp.einsum("nthe,nshe->hnts", query_blk, keys_blk, preferred_element_type=jnp.float32)
    weights_bf = (scores * decay_w).astype(jnp.bfloat16)
    intra = jnp.einsum(
        "hnts,nshe->nthe", weights_bf, values_blk, preferred_element_type=jnp.float32
    )
    carry_out = jnp.where(later_start[None], 0.0, jnp.exp(running[:, :, -1:] - running))
    weighted = (keys_blk * jnp.transpose(carry_out, (1, 2, 0))[..., None]).astype(jnp.bfloat16)
    block_update = jnp.einsum(
        "nshd,nshe->nhde", weighted, values_blk, preferred_element_type=jnp.float32
    )
    block_decay = jnp.where(started[:, -1][None], 0.0, jnp.exp(running[:, :, -1]))
    enter_decay = jnp.where(started[None], 0.0, jnp.exp(running))
    return (intra, enter_decay, block_update, block_decay)


def block_states(block_update, block_decay):

    def advance(carried_in, inputs):
        current, product = carried_in
        one_update, one_decay = inputs
        return (
            (one_decay[:, None, None] * current + one_update, product * one_decay),
            (current, product),
        )

    initial = (
        jnp.zeros(block_update.shape[1:], jnp.float32),
        jnp.ones((block_decay.shape[0],), jnp.float32),
    )
    outcome, history = lax.scan(advance, initial, (block_update, jnp.transpose(block_decay)))
    return (history[0], history[1], outcome[0], outcome[1])


def finish(query, intra, enter_decay, states, norm_gain):
    blocks, block_len, heads_here, head_size = intra.shape
    query_blk = query.reshape(blocks, block_len, heads_here, head_size)
    carried = jnp.einsum(
        "nthe,nhef->nthf",
        query_blk,
        states.astype(jnp.bfloat16),
        preferred_element_type=jnp.float32,
    )
    attended = intra + carried * jnp.transpose(enter_decay, (1, 2, 0))[..., None]
    inv_rms = lax.rsqrt(jnp.mean(attended * attended, axis=-1, keepdims=True) + 1e-06)
    result = (attended * inv_rms * norm_gain[None, None, :, :]).astype(jnp.bfloat16)
    return result.reshape(blocks * block_len, heads_here, head_size)


def combine(earlier, latter):
    return (earlier[0] * latter[0], latter[0][:, None, None] * earlier[1] + latter[1])


def body(tokens, w_query, w_key, w_value, norm_gain, log_decay, lengths):
    rows_here = tokens.shape[0]
    heads_here = w_query.shape[0]
    head_size = w_query.shape[2]
    block_len = BLOCK
    pieces = (
        lax.all_gather(w_query, "seq", axis=1, tiled=True),
        lax.all_gather(w_key, "seq", axis=1, tiled=True),
        lax.all_gather(w_value, "seq", axis=1, tiled=True),
    )
    sums = tuple(
        (
            jnp.einsum("td,hde->the", tokens, weight_mat, preferred_element_type=jnp.float32)
            for weight_mat in pieces
        )
    )
    query = sums[0].astype(jnp.bfloat16)
    keys = sums[1].astype(jnp.bfloat16)
    value_rows = sums[2].astype(jnp.bfloat16)
    first_pos = lax.axis_index("seq") * rows_here
    is_start, segment = segment_info(lengths, first_pos, rows_here)
    intra, enter_decay, block_update, block_decay = local_blocks(
        query, keys, value_rows, log_decay, is_start, segment, block_len
    )
    zero_states, prefix, last_state, shard_decay = block_states(block_update, block_decay)
    identity = (
        jnp.ones((heads_here,), jnp.float32),
        jnp.zeros((heads_here, head_size, head_size), jnp.float32),
    )
    incoming = entering((shard_decay, last_state), "seq", combine, identity)
    states = prefix[:, :, None, None] * incoming[1][None] + zero_states
    return finish(query, intra, enter_decay, states, norm_gain)


def solution(mesh):
    return jax.shard_map(
        body,
        mesh=mesh,
        in_specs=(
            P(("groups", "seq"), None),
            P("head", "seq", None),
            P("head", "seq", None),
            P("head", "seq", None),
            P("head", None),
            P("head", ("groups", "seq")),
            P("groups"),
        ),
        out_specs=P(("groups", "seq"), "head", None),
        check_vma=False,
    )
```

profile of v0, /device:TPU:0, one launch (start us, length us, event | category | flops | bytes accessed | tf_op | source)
XLA Modules:
  0.0 703.9 jit_solution(5788084500042480428)
XLA Ops:
  11.4 177.3 %all-gather.11.cloned.1.call-done = bf16[16,3072,128]{2,1,0:T(8,128)(2,1)} async-done(((bf16[16,384,128]{2,1,0:T(8,128)(2,1)}), bf16[16,3072,128]{2,1,0:T(8,128)(2,1)}) %all-gather.11.cloned.1.call-update) | async-done | bytes 12582928 | tf_op jit(solution)/shard_map/all_gather | solution.py:110
  188.7 10.6 %fusion.21 = bf16[512,16,128]{2,0,1:T(8,128)(2,1)} fusion(bf16[16,3072,128]{2,1,0:T(8,128)(2,1)} %all-gather.11.cloned.1.call-done, bf16[512,3072]{1,0:T(8,128)(2,1)S(1)} %copy-done), kind=kOutput, calls=%fused_computation.29 | convolution fusion | flops 6443499520 | bytes 17825792 | tf_op jit(solution)/shard_map/td,hde->the/dot_general | solution.py:115
  199.3 4.1 copy.31
  203.5 162.1 %all-gather.7.cloned.1.call-done = bf16[16,3072,128]{2,1,0:T(8,128)(2,1)} async-done(((bf16[16,384,128]{2,1,0:T(8,128)(2,1)}), bf16[16,3072,128]{2,1,0:T(8,128)(2,1)}) %all-gather.7.cloned.1.call-update) | async-done | bytes 12582928 | tf_op jit(solution)/shard_map/all_gather | solution.py:111
  365.6 9.8 %fusion.15 = bf16[512,16,128]{2,0,1:T(8,128)(2,1)S(1)} fusion(bf16[16,3072,128]{2,1,0:T(8,128)(2,1)} %all-gather.7.cloned.1.call-done, bf16[512,3072]{1,0:T(8,128)(2,1)S(1)} %copy-done), kind=kOutput, calls=%fused_computation.27 | convolution fusion | flops 6443499520 | bytes 17825792 | tf_op jit(solution)/shard_map/td,hde->the/dot_general | solution.py:115
  375.4 2.7 fusion.11
  378.1 18.7 %while.31 = (s32[]{:T(128)}, f32[16,128,128]{2,1,0:T(8,128)}, f32[16]{0:T(128)S(1)}, f32[4,16,128,128]{3,2,1,0:T(8,128)}, f32[4,16]{1,0:T(4,128)S(1)}, /*index=5...) while((s32[]{:T(128)}, f32[16,128,128]{2,1,0:T(8,128)}, ...), condition=%wide.region_6.7_spmd.clone, body=%wide.region_5.6_spmd.clone.sunk | while | flops 1048611 | bytes 5243521 | solution.py:80
  383.9 2.7 bitcast_add_fusion.3
  389.0 2.7 bitcast_add_fusion.3
  394.0 2.7 bitcast_add_fusion.3
  398.5 19.9 %all-reduce = f32[128]{0:T(128)S(1)} all-reduce(f32[128]{0:T(128)S(1)} %dynamic-update-slice), channel_id=2, replica_groups=mesh['groups'=2,'seq'=8,'head'=2] {'seq'}, use_global_device_ids=true, to_apply=%add | all-reduce | flops 128 | bytes 1024
  418.6 124.1 %all-gather.9.cloned.1.call-done = bf16[16,3072,128]{2,1,0:T(8,128)(2,1)} async-done(((bf16[16,384,128]{2,1,0:T(8,128)(2,1)}), bf16[16,3072,128]{2,1,0:T(8,128)(2,1)}) %all-gather.9.cloned.1.call-update) | async-done | bytes 12582928 | tf_op jit(solution)/shard_map/all_gather | solution.py:109
  542.7 10.6 %fusion.18 = bf16[512,16,128]{2,0,1:T(8,128)(2,1)} fusion(bf16[16,3072,128]{2,1,0:T(8,128)(2,1)} %all-gather.9.cloned.1.call-done, bf16[512,3072]{1,0:T(8,128)(2,1)S(1)} %copy-done), kind=kOutput, calls=%fused_computation.28 | convolution fusion | flops 6443499520 | bytes 17825792 | tf_op jit(solution)/shard_map/td,hde->the/dot_general | solution.py:115
  553.3 5.0 fusion.25
  558.3 109.5 %all-gather.13.cloned.1.call-done = f32[128,128,128]{2,1,0:T(8,128)} async-done(((f32[16,128,128]{2,1,0:T(8,128)}), f32[128,128,128]{2,1,0:T(8,128)}) %all-gather.13.cloned.1.call-update) | async-done | bytes 8388624 | tf_op jit(solution)/shard_map/all_gather | solution.py:11
  667.8 18.9 %while.32 = (s32[]{:T(128)}, f32[16,128,128]{2,1,0:T(8,128)}, s32[]{:T(128)}, f32[8,16]{1,0:T(8,128)S(1)}, f32[8,16,128,128]{3,2,1,0:T(8,128)}, /*index=5*/s32[]{:T(128)}, s32[]{:T(128)}) while((s32[]{:T(128)}, f32[16,128,128]{2,1,0:T(8,128)}, s32[]{:T(128)}, f32[8,16]{1,0:T(8,128)S(1)}, f32[8,16,128,128]{3,2,1,0:T(8,128)}, ...), condition=%wide.region_8.9_spmd.clone, body=%wide.region_7.8_spmd.clone.sunk | while | flops 1048580 | bytes 3146033 | solution.py:20
  670.2 2.7 fusion.43
  673.0 2.7 fusion.43
  675.7 2.7 fusion.43
  678.5 2.7 fusion.43
  681.2 2.7 fusion.43
  683.9 2.7 fusion.43
  686.7 6.7 multiply_reduce_fusion
  694.7 2.7 copy.34
  (71 shorter events, 20.2 us)
Async XLA Ops:
  6.5 182.2 %copy-start = (bf16[512,3072]{1,0:T(8,128)(2,1)S(1)}, bf16[512,3072]{1,0:T(8,128)(2,1)}, u32[]{:S(2)}) copy-start(bf16[512,3072]{1,0:T(8,128)(2,1)} %param.11) | copy-start | bytes 9437188
  6.5 2.3 copy-start.5
  6.5 2.9 copy-start.3
  6.5 182.2 %all-gather.11.cloned.1.call-start = ((), (), s32[]{:S(2)}) async-start(), calls=%async_computation.2 | async-start | bytes 14155776 | tf_op jit(solution)/shard_map/all_gather | solution.py:110
  7.3 358.3 %all-gather.7.cloned.1.call-start = ((), (), s32[]{:S(2)}) async-start(), calls=%async_computation | async-start | bytes 14155776 | tf_op jit(solution)/shard_map/all_gather | solution.py:111
  8.0 534.7 %all-gather.9.cloned.1.call-start = ((), (), s32[]{:S(2)}) async-start(), calls=%async_computation.1 | async-start | bytes 14155776 | tf_op jit(solution)/shard_map/all_gather | solution.py:109
  8.7 659.1 %all-gather.13.cloned.1.call-start = ((), (), s32[]{:S(2)}) async-start(), calls=%async_computation.3 | async-start | bytes 9437184 | tf_op jit(solution)/shard_map/all_gather | solution.py:11
  365.6 9.8 %copy-start.1 = (bf16[4,128,16,128]{1,3,2,0:T(8,128)(2,1)S(1)}, bf16[4,128,16,128]{1,3,2,0:T(8,128)(2,1)}, u32[]{:S(2)}) copy-start(bf16[4,128,16,128]{1,3,2,0:T(8,128)(2,1)} %copy.31) | copy-start | bytes 6291460
  375.4 2.7 copy-start.2
  378.1 18.7 %copy-start.6 = (u32[32]{0:T(128)S(1)}, u32[32]{0:T(128)}, u32[]{:S(2)}) copy-start(u32[32]{0:T(128)} %constant.71) | copy-start | bytes 388
  686.7 6.8 copy-start.4
Sparse Core Ops, SparseCore 0:
  9.6 179.1 all-gather.10
  190.9 174.6 all-gather.6
  367.8 174.8 all-gather.8
  544.7 123.1 all-gather.12
where the time goes:
time: 705 us; the launch traced here: 704 us
  waiting for transfers between devices  575 us (82%)
  matrix products  45.4 us (6%)
  other arithmetic  40.9 us (6%)
  blocking collectives  19.9 us (3%)
  between operations  14 us (2%)
  local copies, waits for them, and re-layouts  8.45 us (1%)
    all_gather x1, waiting for transfers between devices, body(): lax.all_gather(w_key, 'seq', axis=1, tiled=True)  177 us
    all_gather x1, waiting for transfers between devices, body(): lax.all_gather(w_value, 'seq', axis=1, tiled=True)  162 us
    all_gather x1, waiting for transfers between devices, body(): lax.all_gather(w_query, 'seq', axis=1, tiled=True)  124 us
    all_gather x1, waiting for transfers between devices, entering(): pieces = jax.tree.map(lambda part: lax.all_gather(part, axis), value)  110 us
    dot_general x3, matrix products, body(): jnp.einsum('td,hde->the', tokens, weight_mat, preferred_element_type=jnp....  31 us
    unnamed x1, blocking collectives  19.9 us
    select_n x7, other arithmetic, step(): jnp.where(position < mine, new, old)  18.8 us
  transfers between devices with their start and end apart: 4, of which 4 were waited for; matrix products, arithmetic and copies ran while one was open for 9% of the time, Pallas kernels for 0%

commit v1 on v0

v1 whole, which is shorter than its diff:
```python
import functools

import jax
import jax.numpy as jnp
from jax import lax
from jax.experimental import pallas as pl
from jax.experimental.pallas import tpu as pltpu
from jax.sharding import PartitionSpec as P

BLOCK = 128
NT = (((1,), (1,)), ((), ()))
TN = (((0,), (0,)), ((), ()))
F32 = jnp.float32
BF16 = jnp.bfloat16


def attend_block(q, k, v, decay, seg, state, gain, consts):
    lower, upper, above = consts
    visible, entered, leaves, passes = seg
    size = q.shape[0]
    rows = jnp.broadcast_to(decay, (size, size))
    gap = lax.dot_general(lower, jnp.where(above, rows, 0), NT, preferred_element_type=F32)
    running = lax.dot_general(lower, rows, NT, preferred_element_type=F32)
    rest = lax.dot_general(upper, rows, NT, preferred_element_type=F32)
    scores = lax.dot_general(q, k, NT, preferred_element_type=F32)
    weights = (scores * jnp.where(visible, jnp.exp(gap), 0.0)).astype(BF16)
    intra = jnp.dot(weights, v, preferred_element_type=F32)
    enter = jnp.where(entered, 0.0, jnp.exp(running))
    carried = jnp.dot(q, state.astype(BF16), preferred_element_type=F32)
    attended = intra + enter * carried
    inv = lax.rsqrt(jnp.mean(attended * attended, axis=1, keepdims=True) + 1e-06)
    out = (attended * inv * gain).astype(BF16)
    carry = jnp.where(leaves, 0.0, jnp.exp(rest))
    weighted = (k.astype(F32) * carry).astype(BF16)
    update = lax.dot_general(weighted, v, TN, preferred_element_type=F32)
    keep = jnp.where(passes, jnp.exp(running[size - 1 : size, :]), 0.0)
    return out, keep * state + update


def segment_of(position, lens_ref, base, prompts):
    end = jnp.int32(0)
    total = 0 * position
    for j in range(prompts):
        end = end + lens_ref[base + j]
        total = total + jnp.where(position >= end, 1, 0)
    return total


def kernel(prompts, lens_ref, tok_ref, w_ref, ld_ref, gain_ref, out_ref, state_ref):
    step = pl.program_id(0)
    heads = ld_ref.shape[0]
    rows = tok_ref.shape[0]
    size = gain_ref.shape[1]

    @pl.when(step == 0)
    def _():
        state_ref[...] = jnp.zeros_like(state_ref)

    qkv = jnp.dot(tok_ref[...], w_ref[...], preferred_element_type=F32).astype(BF16)
    ti = lax.broadcasted_iota(jnp.int32, (BLOCK, BLOCK), 0)
    si = lax.broadcasted_iota(jnp.int32, (BLOCK, BLOCK), 1)
    consts = ((ti >= si).astype(F32).astype(BF16), (ti < si).astype(F32).astype(BF16), ti < si)
    for b in range(rows // BLOCK):
        first = (step * rows + b * BLOCK).astype(jnp.int32)
        seg_t = segment_of(first + ti, lens_ref, 0, prompts)
        seg_s = segment_of(first + si, lens_ref, 0, prompts)
        seg_before = segment_of(first - 1, lens_ref, 0, prompts)
        seg_last = segment_of(first + BLOCK - 1, lens_ref, 0, prompts)
        seg_before = jnp.where(first == 0, -1, seg_before)
        seg = (
            (ti >= si) & (seg_t == seg_s),
            seg_t != seg_before,
            seg_t != seg_last,
            seg_before == seg_last,
        )
        here = slice(b * BLOCK, (b + 1) * BLOCK)
        for h in range(heads):
            part = [qkv[here, (i * heads + h) * size : (i * heads + h + 1) * size] for i in range(3)]
            out, state = attend_block(
                *part, ld_ref[h : h + 1, here], seg, state_ref[h], gain_ref[h : h + 1, :], consts
            )
            state_ref[h] = state
            out_ref[here, h * size : (h + 1) * size] = out


def body(tokens, w_query, w_key, w_value, norm_gain, log_decay, lengths):
    rows_here, width = tokens.shape
    heads_here, depth, size = w_query.shape
    count = lax.axis_size("seq")
    mine = heads_here // count
    cores = lax.axis_size("head")
    part = width // cores
    half = lax.dynamic_slice(tokens, (0, lax.axis_index("head") * part), (rows_here, part))
    gathered = lax.all_gather(half, "seq", axis=0, tiled=True)
    everyone = lax.all_gather(gathered, "head", axis=1, tiled=True)
    stacked = jnp.stack([w_query, w_key, w_value])
    moved = lax.all_to_all(stacked, "seq", split_axis=1, concat_axis=2, tiled=True)
    weights = jnp.transpose(moved, (2, 0, 1, 3)).reshape(width, 3 * mine * size)
    decays = lax.all_gather(log_decay, "seq", axis=1, tiled=True)
    first_head = lax.axis_index("seq") * mine
    decays = lax.dynamic_slice_in_dim(decays, first_head, mine, axis=0)
    gains = lax.dynamic_slice_in_dim(norm_gain, first_head, mine, axis=0)
    total = rows_here * count
    out = pl.pallas_call(
        functools.partial(kernel, lengths.shape[0]),
        grid=(count,),
        out_shape=jax.ShapeDtypeStruct((total, mine * size), BF16),
        in_specs=[
            pl.BlockSpec(memory_space=pltpu.SMEM),
            pl.BlockSpec((rows_here, width), lambda i: (i, 0)),
            pl.BlockSpec((width, 3 * mine * size), lambda i: (0, 0)),
            pl.BlockSpec((mine, rows_here), lambda i: (0, i)),
            pl.BlockSpec((mine, size), lambda i: (0, 0)),
        ],
        out_specs=pl.BlockSpec((rows_here, mine * size), lambda i: (i, 0)),
        scratch_shapes=[pltpu.VMEM((mine, size, size), F32)],
        compiler_params=pltpu.CompilerParams(vmem_limit_bytes=48 * 2**20),
    )(lengths, everyone, weights, decays, gains)
    back = lax.all_to_all(out, "seq", split_axis=0, concat_axis=1, tiled=True)
    return back.reshape(rows_here, heads_here, size)


def solution(mesh):
    return jax.shard_map(
        body,
        mesh=mesh,
        in_specs=(
            P(("groups", "seq"), None),
            P("head", "seq", None),
            P("head", "seq", None),
            P("head", "seq", None),
            P("head", None),
            P("head", ("groups", "seq")),
            P("groups"),
        ),
        out_specs=P(("groups", "seq"), "head", None),
        check_vma=False,
    )
```

time: 705 us -> 453 us (0.64)
  waiting for transfers between devices: 575 us -> 179 us
  blocking collectives: 19.9 us -> 170 us
  Pallas kernels: 0 us -> 48 us
  matrix products: 45.4 us -> 0 us
  other arithmetic: 40.9 us -> 3.64 us
  local copies, waits for them, and re-layouts: 8.45 us -> 33.1 us
    all_gather x4 -> x2, waiting for transfers between devices: 573 us -> 179 us  [the longest x1 179 us: body(): gathered = lax.all_gather(half, 'seq', axis=0, tiled=True)]
    all_gather x0 -> x1, blocking collectives: none -> 124 us  [body(): decays = lax.all_gather(log_decay, 'seq', axis=1, tiled=True)]
    pallas_call x0 -> x1, Pallas kernels: none -> 48 us  [body(): pl.pallas_call(functools.partial(kernel, lengths.shape[0]), grid=(count,)...]
    all_to_all x0 -> x1, blocking collectives: none -> 45.6 us  [body(): back = lax.all_to_all(out, 'seq', split_axis=0, concat_axis=1, tiled=True)]
    dot_general x6 -> x0, matrix products: 45.4 us -> none  [the longest x3 31 us: body(): jnp.einsum('td,hde->the', tokens, weight_mat, preferred_element_type=jnp....]
    unnamed x1 -> x0, blocking collectives: 19.9 us -> none
    select_n x8 -> x0, other arithmetic: 18.9 us -> none  [the longest x7 18.8 us: step(): jnp.where(position < mine, new, old)]
    all_to_all x0 -> x2, local copies, waits for them, and re-layouts: none -> 11.9 us  [the longest x1 9.41 us: body(): lax.all_to_all(stacked, 'seq', split_axis=1, concat_axis=2, tiled=True)]
  transfers between devices with their start and end apart: 4 -> 3, of which waited for: 4 -> 1; matrix products, arithmetic and copies ran while one was open for 9% -> 6% of each run, Pallas kernels for 0% -> 0%
where the time goes in v1:
time: 453 us; the launch traced here: 452 us
  waiting for transfers between devices  179 us (40%)
  blocking collectives  170 us (38%)
  Pallas kernels  48 us (11%)
  local copies, waits for them, and re-layouts  33.1 us (7%)
  between operations  13.4 us (3%)
  starting transfers between devices  4.93 us (1%)
    all_gather x1, waiting for transfers between devices, body(): gathered = lax.all_gather(half, 'seq', axis=0, tiled=True)  179 us
    all_gather x1, blocking collectives, body(): decays = lax.all_gather(log_decay, 'seq', axis=1, tiled=True)  124 us
    pallas_call x1, Pallas kernels, body(): pl.pallas_call(functools.partial(kernel, lengths.shape[0]), grid=(count,)...  48 us
    all_to_all x1, blocking collectives, body(): back = lax.all_to_all(out, 'seq', split_axis=0, concat_axis=1, tiled=True)  45.6 us
    reshape x1, local copies, waits for them, and re-layouts, body(): weights = jnp.transpose(moved, (2, 0, 1, 3)).reshape(width, 3 * mine * size)  11.4 us
    all_to_all x1, local copies, waits for them, and re-layouts, body(): lax.all_to_all(stacked, 'seq', split_axis=1, concat_axis=2, tiled=True)  9.41 us
  transfers between devices with their start and end apart: 3, of which 1 were waited for; matrix products, arithmetic and copies ran while one was open for 6% of the time, Pallas kernels for 0%

profile of v1, /device:TPU:0, one launch (start us, length us, event | category | flops | bytes accessed | tf_op | source)
XLA Modules:
  0.0 452.2 jit_solution(5790718785236989929)
XLA Ops:
  6.5 0.0 copy-start
  6.5 0.0 all-gather.3.cloned.1.call-start
  6.5 1.9 copy-done
  8.4 1.2 constant_dynamic-slice_fusion.2
  9.7 0.0 all-gather.3.cloned.1.call-update
  9.7 0.0 all-gather.5.cloned.1.call-start
  9.7 179.2 %all-gather.3.cloned.1.call-done = bf16[4096,1536]{1,0:T(8,128)(2,1)} async-done(((bf16[512,1536]{1,0:T(8,128)(2,1)}), bf16[4096,1536]{1,0:T(8,128)(2,1)}) %all-gather.3.cloned.1.call-update) | async-done | bytes 12582928 | tf_op jit(solution)/shard_map/all_gather | solution.py:94
  189.0 0.0 all-gather.5.cloned.1.call-update
  189.0 1.4 copy-done.3
  190.4 0.5 copy-done.4
  190.9 3.6 pad_maximum_fusion
  194.5 4.9 %all-to-all-start = ((bf16[3,16,384,128]{3,2,0,1:T(8,128)(2,1)}), bf16[3,16,384,128]{3,2,0,1:T(8,128)(2,1)}, u32[]{:S(2)}, u32[]{:S(2)}) async-start(bf16[3,16,384,128]{3,2,0,1:T(8,128)(2,1)} %pad_maximum_fusion), calls=%async_computation | async-start | bytes 9437184 | tf_op jit(solution)/shard_map/all_to_all | solution.py:97
  199.4 0.0 copy-done.5
  199.4 124.2 %all_gather.11 = bf16[16,4096]{1,0:T(8,128)(2,1)S(1)} all-gather(bf16[16,512]{1,0:T(8,128)(2,1)S(1)} %copy-done.5), channel_id=1, replica_groups=mesh['groups'=2,'seq'=8,'head'=2] {'seq'}, dimensions={1}, use_global_device_ids=true | all-gather | bytes 147456 | tf_op jit(solution)/shard_map/all_gather | solution.py:99
  323.7 0.7 constant_dynamic-slice_fusion.gain_ref
  324.4 0.0 all-to-all-done
  324.4 9.4 %copy.10 = bf16[3,2,8,384,128]{4,1,0,3,2:T(2,128)(2,1)} copy(bf16[3,2,8,384,128]{4,3,0,1,2:T(8,128)(2,1)} %bitcast.4) | data formatting | bytes 9437184 | tf_op jit(solution)/shard_map/all_to_all | solution.py:97
  333.8 11.4 %reshape.10.w_ref = bf16[3072,768]{1,0:T(8,128)(2,1)} reshape(bf16[3072,3,2,128]{3,2,1,0:T(2,128)(2,1)} %bitcast.12) | data formatting | bytes 9437184 | tf_op jit(solution)/shard_map/reshape | solution.py:98
  345.2 0.0 copy-done.2
  345.2 48.0 %shard_map.73 = bf16[4096,256]{1,0:T(8,128)(2,1)S(1)} custom-call(s32[4]{0:T(128)S(1)} %copy-done.2, bf16[4096,3072]{1,0:T(8,128)(2,1)} %all-gather.5.cloned.1.call-done.tok_ref, bf16[3072,768]{1,0:T(8,128)(2,1)} %reshape.10.w_ref, bf16[2,4096]{1,0:T(2,128)(2,1)S(1)} %constant_dynamic-slice_fusion.1.ld_ref, f32[2,128]{1,0:T(2,128)S(1)} %constant_dynamic-slice_fusion.gain_ref), custom_call_target="tpu_custom_call" | custom-call | tf_op jit(solution)/shard_map/pallas_call | solution.py:104
  393.2 45.6 %all_to_all.34 = bf16[8,512,256]{2,1,0:T(8,128)(2,1)S(1)} all-to-all(bf16[8,512,256]{2,1,0:T(8,128)(2,1)S(1)} %bitcast.11), channel_id=1, replica_groups=mesh['groups'=2,'seq'=8,'head'=2] {'seq'}, dimensions={0} | all-to-all | bytes 4194304 | tf_op jit(solution)/shard_map/all_to_all | solution.py:119
  438.8 2.5 copy.11
  441.3 4.1 reshape.11
  445.4 0.0 copy-done.1
  (7 shorter events, 0.0 us)
Async XLA Ops:
  6.5 1.9 copy-start
  6.5 182.4 %all-gather.3.cloned.1.call-start = ((), (), s32[]{:S(2)}) async-start(), calls=%async_computation.2 | async-start | bytes 14155776 | tf_op jit(solution)/shard_map/all_gather | solution.py:94
  9.7 335.5 %all-gather.5.cloned.1.call-start = ((), (), s32[]{:S(2)}) async-start(), calls=%async_computation.3 | async-start | bytes 37748736 | tf_op jit(solution)/shard_map/all_gather | solution.py:95
  189.0 1.4 copy-start.3
  189.0 1.9 copy-start.4
  194.5 4.9 %copy-start.5 = (bf16[16,512]{1,0:T(8,128)(2,1)S(1)}, bf16[16,512]{1,0:T(8,128)(2,1)}, u32[]{:S(2)}) copy-start(bf16[16,512]{1,0:T(8,128)(2,1)} %param.12) | copy-start | bytes 49156
  194.5 129.9 %all-to-all-start = ((bf16[3,16,384,128]{3,2,0,1:T(8,128)(2,1)}), bf16[3,16,384,128]{3,2,0,1:T(8,128)(2,1)}, u32[]{:S(2)}, u32[]{:S(2)}) async-start(bf16[3,16,384,128]{3,2,0,1:T(8,128)(2,1)} %pad_maximum_fusion), calls=%async_computation | async-start | bytes 9437184 | tf_op jit(solution)/shard_map/all_to_all | solution.py:97
  333.8 11.4 %copy-start.2 = (s32[4]{0:T(128)S(1)}, s32[4]{0:T(128)}, u32[]{:S(2)}) copy-start(s32[4]{0:T(128)} %lens_ref.1) | copy-start | bytes 52
  438.8 6.6 %copy-start.1 = (bf16[512,3072]{1,0:T(8,128)(2,1)S(1)}, bf16[512,3072]{1,0:T(8,128)(2,1)}, u32[]{:S(2)}) copy-start(bf16[512,3072]{1,0:T(8,128)(2,1)} %param.7) | copy-start | bytes 9437188
Sparse Core Ops, SparseCore 0:
  9.8 179.1 all-gather.2
  190.5 40.6 all-gather.4

commit v2 on v1

--- a/solution.py
+++ b/solution.py
@@ -12,6 +12,7 @@
 TN = (((0,), (0,)), ((), ()))
 F32 = jnp.float32
 BF16 = jnp.bfloat16
+MESH = pl.DeviceIdType.MESH
 
 
 def attend_block(q, k, v, decay, seg, state, gain, consts):
@@ -46,17 +47,16 @@
     return total
 
 
-def kernel(prompts, lens_ref, tok_ref, w_ref, ld_ref, gain_ref, out_ref, state_ref):
+def attend_kernel(prompts, lens_ref, qkv_ref, ld_ref, gain_ref, out_ref, state_ref):
     step = pl.program_id(0)
     heads = ld_ref.shape[0]
-    rows = tok_ref.shape[0]
+    rows = qkv_ref.shape[0]
     size = gain_ref.shape[1]
 
     @pl.when(step == 0)
     def _():
         state_ref[...] = jnp.zeros_like(state_ref)
 
-    qkv = jnp.dot(tok_ref[...], w_ref[...], preferred_element_type=F32).astype(BF16)
     ti = lax.broadcasted_iota(jnp.int32, (BLOCK, BLOCK), 0)
     si = lax.broadcasted_iota(jnp.int32, (BLOCK, BLOCK), 1)
     consts = ((ti >= si).astype(F32).astype(BF16), (ti < si).astype(F32).astype(BF16), ti < si)
@@ -75,7 +75,7 @@
         )
         here = slice(b * BLOCK, (b + 1) * BLOCK)
         for h in range(heads):
-            part = [qkv[here, (i * heads + h) * size : (i * heads + h + 1) * size] for i in range(3)]
+            part = [qkv_ref[here, (i * heads + h) * size : (i * heads + h + 1) * size] for i in range(3)]
             out, state = attend_block(
                 *part, ld_ref[h : h + 1, here], seg, state_ref[h], gain_ref[h : h + 1, :], consts
             )
@@ -83,39 +83,270 @@
             out_ref[here, h * size : (h + 1) * size] = out
 
 
-def body(tokens, w_query, w_key, w_value, norm_gain, log_decay, lengths):
+def gather_kernel(
+    inner, tok_hbm, wq, wk, wv, out_ref, tok, landed, joined,
+    own_sem, w_own, z_send, y_send, core_send, tok_recv, w_send, w_recv,
+):
+    count = lax.axis_size("seq")
+    outer = count // inner
+    me, core, group = lax.axis_index("seq"), lax.axis_index("head"), lax.axis_index("groups")
+    far, near = me // inner, me % inner
+    weights = (wq, wk, wv)
+    mine, depth = wq.shape[0] // count, wq.shape[1]
+    part = depth // 2
+    side = group % 2
+    rows = tok.shape[2]
+    size = wq.shape[2]
+    other_core = {"head": 1 - core}
+    twin = {"groups": group + 1 - 2 * side}
+
+    barrier = pltpu.get_barrier_semaphore()
+    for i in range(1, count):
+        pl.semaphore_signal(barrier, device_id={"seq": (me + i) % count}, device_id_type=MESH)
+    pl.semaphore_signal(barrier, device_id=other_core, device_id_type=MESH)
+    pl.semaphore_signal(barrier, device_id=twin, device_id_type=MESH)
+    pl.semaphore_wait(barrier, count + 1)
+
+    def own_copy(h):
+        return pltpu.make_async_copy(tok_hbm.at[pl.ds(h * rows, rows)], tok.at[me, h], own_sem.at[h])
+
+    def own_weights(m):
+        return pltpu.make_async_copy(
+            weights[m].at[pl.ds(me * mine, mine)],
+            landed.at[m, :, pl.ds(pl.multiple_of(me * depth, 16), depth)],
+            w_own.at[m],
+        )
+
+    def remote(src, dst, send, recv, device):
+        return pltpu.make_async_remote_copy(
+            src_ref=src, dst_ref=dst, send_sem=send, recv_sem=recv, device_id=device, device_id_type=MESH
+        )
+
+    def shard(s, h, send, device):
+        return remote(tok.at[s, h], tok.at[s, h], send, tok_recv.at[s, h], device)
+
+    def slot(m, s, half):
+        start = pl.multiple_of(s * depth + half * part, 16)
+        return landed.at[m, :, pl.ds(start, part)]
+
+    def weight_out(m, i):
+        to = (me + i) % count
+        src = weights[m].at[pl.ds(to * mine, mine), pl.ds(pl.multiple_of(side * part, 16), part)]
+        return remote(src, slot(m, me, side), w_send.at[0, i, m], w_recv.at[side, me, m], {"seq": to})
+
+    def weight_over(m, i):
+        s = (me + count - i) % count
+        return remote(slot(m, s, side), slot(m, s, side), w_send.at[1, i, m], w_recv.at[side, s, m], twin)
+
+    def weight_in(m, i, half):
+        s = (me + count - i) % count
+        return remote(slot(m, s, half), slot(m, s, half), w_send.at[1, i, m], w_recv.at[half, s, m], twin)
+
+    for h in range(2):
+        own_copy(h).start()
+    for m in range(3):
+        own_weights(m).start()
+    for h in range(2):
+        own_copy(h).wait()
+
+    def forwards(j, act):
+        step = (j + 1) // 2
+        offset = jnp.where(j % 2 == 1, -step, step)
+        place = far + offset
+        s = place * inner + near
+        inside = (place >= 0) & (place < outer)
+
+        @pl.when(inside & (offset <= 0) & (far + 1 < outer))
+        def _():
+            act(shard(s, core, z_send.at[0, j], {"seq": me + inner}))
+
+        @pl.when(inside & (offset >= 0) & (far > 0))
+        def _():
+            act(shard(s, core, z_send.at[1, j], {"seq": me - inner}))
+
+        for k in range(1, inner):
+            @pl.when(inside)
+            def _():
+                act(shard(s, core, y_send.at[k, j], {"seq": far * inner + (near + k) % inner}))
+
+        @pl.when(inside & (j > 0))
+        def _():
+            act(shard(s, core, core_send.at[0, j], other_core))
+
+    def crossing(j, act):
+        step = (j + 1) // 2
+        place = far + jnp.where(j % 2 == 1, -step, step)
+        for k in range(1, inner):
+            s = place * inner + (near + k) % inner
+
+            @pl.when((place >= 0) & (place < outer))
+            def _():
+                act(shard(s, core, core_send.at[k, j], other_core), s)
+
+    def arrived(s, h):
+        shard(s, h, own_sem.at[0], other_core).wait_recv()
+
+    def receive_and_start(copy, s):
+        arrived(s, core)
+        copy.start()
+
+    forwards(0, lambda copy: copy.start())
+    for i in range(1, count):
+        for m in range(3):
+            weight_out(m, i).start()
+
+    last = 2 * outer - 1
+
+    def serve(j, carry):
+        step = (j + 1) // 2
+        place = far + jnp.where(j % 2 == 1, -step, step)
+
+        @pl.when((j < last) & (place >= 0) & (place < outer))
+        def _():
+            arrived(place * inner + near, core)
+
+        @pl.when(j < last)
+        def _():
+            forwards(j, lambda copy: copy.start())
+
+        @pl.when(j >= 2)
+        def _():
+            crossing(j - 2, receive_and_start)
+
+        for k in range(2):
+            i = 2 * (j - 3) + 1 + k
+
+            @pl.when((i >= 1) & (i < count))
+            def _():
+                for m in range(3):
+                    weight_in(m, i, side).wait_recv()
+                    weight_over(m, i).start()
+
+        return carry
+
+    lax.fori_loop(1, last + 2, serve, 0)
+
+    for m in range(3):
+        own_weights(m).wait()
+    for i in range(1, count):
+        for m in range(3):
+            weight_in(m, i, 1 - side).wait_recv()
+
+    def join(s, carry):
+        here = pl.ds(pl.multiple_of(s * depth, 16), depth)
+        for m in range(3):
+            for h in range(mine):
+                at = (m * mine + h) * size
+                joined[here, at : at + size] = landed[m, h, here, :]
+        return carry
+
+    lax.fori_loop(0, count, join, 0)
+
+    def project(i, carry):
+        s = (me + i) % count
+
+        @pl.when(i > 0)
+        def _():
+            arrived(s, 1 - core)
+
+        for h in range(2):
+            start = pl.multiple_of((2 * s + h) * rows, 16)
+            out_ref[pl.ds(start, rows), :] = jnp.dot(
+                tok[s, h], joined[...], preferred_element_type=F32
+            ).astype(BF16)
+        return carry
+
+    lax.fori_loop(0, count, project, 0)
+
+    def drain(j, carry):
+        forwards(j, lambda copy: copy.wait_send())
+        crossing(j, lambda copy, s: copy.wait_send())
+        return carry
+
+    lax.fori_loop(0, last, drain, 0)
+    for i in range(1, count):
+        for m in range(3):
+            weight_out(m, i).wait_send()
+            weight_over(m, i).wait_send()
+
+
+def project_remote(inner, tokens, w_query, w_key, w_value):
     rows_here, width = tokens.shape
     heads_here, depth, size = w_query.shape
     count = lax.axis_size("seq")
     mine = heads_here // count
-    cores = lax.axis_size("head")
-    part = width // cores
+    outer = count // inner
+    columns = 3 * mine * size
+    anywhere = pl.BlockSpec(memory_space=pl.ANY)
+    dma = pltpu.SemaphoreType.DMA
+    return pl.pallas_call(
+        functools.partial(gather_kernel, inner),
+        out_shape=jax.ShapeDtypeStruct((rows_here * count, columns), BF16),
+        in_specs=[anywhere] * 4,
+        out_specs=pl.BlockSpec(memory_space=pltpu.VMEM),
+        scratch_shapes=[
+            pltpu.VMEM((count, 2, rows_here // 2, width), BF16),
+            pltpu.VMEM((3, mine, width, size), BF16),
+            pltpu.VMEM((width, columns), BF16),
+            dma((2,)),
+            dma((3,)),
+            dma((2, 2 * outer)),
+            dma((inner, 2 * outer)),
+            dma((inner, 2 * outer)),
+            dma((count, 2)),
+            dma((2, count, 3)),
+            dma((2, count, 3)),
+        ],
+        compiler_params=pltpu.CompilerParams(
+            collective_id=0, has_side_effects=True, vmem_limit_bytes=56 * 2**20
+        ),
+    )(tokens, w_query, w_key, w_value)
+
+
+def project_plain(tokens, w_query, w_key, w_value):
+    rows_here, width = tokens.shape
+    heads_here, depth, size = w_query.shape
+    mine = heads_here // lax.axis_size("seq")
+    part = width // lax.axis_size("head")
     half = lax.dynamic_slice(tokens, (0, lax.axis_index("head") * part), (rows_here, part))
     gathered = lax.all_gather(half, "seq", axis=0, tiled=True)
     everyone = lax.all_gather(gathered, "head", axis=1, tiled=True)
     stacked = jnp.stack([w_query, w_key, w_value])
     moved = lax.all_to_all(stacked, "seq", split_axis=1, concat_axis=2, tiled=True)
     weights = jnp.transpose(moved, (2, 0, 1, 3)).reshape(width, 3 * mine * size)
+    return jnp.dot(everyone, weights, preferred_element_type=F32).astype(BF16)
+
+
+def body(tokens, w_query, w_key, w_value, norm_gain, log_decay, lengths):
+    rows_here, width = tokens.shape
+    heads_here, depth, size = w_query.shape
+    count = lax.axis_size("seq")
+    mine = heads_here // count
+    total = rows_here * count
+    fits = 2 * (total * width + total * 3 * mine * size + 6 * mine * size * width) < 48 * 2**20
+    if fits and lax.axis_size("groups") % 2 == 0 and lax.axis_size("head") == 2:
+        inner = 2 if count % 2 == 0 else 1
+        qkv = project_remote(inner, tokens, w_query, w_key, w_value)
+    else:
+        qkv = project_plain(tokens, w_query, w_key, w_value)
     decays = lax.all_gather(log_decay, "seq", axis=1, tiled=True)
     first_head = lax.axis_index("seq") * mine
     decays = lax.dynamic_slice_in_dim(decays, first_head, mine, axis=0)
     gains = lax.dynamic_slice_in_dim(norm_gain, first_head, mine, axis=0)
-    total = rows_here * count
     out = pl.pallas_call(
-        functools.partial(kernel, lengths.shape[0]),
+        functools.partial(attend_kernel, lengths.shape[0]),
         grid=(count,),
         out_shape=jax.ShapeDtypeStruct((total, mine * size), BF16),
         in_specs=[
             pl.BlockSpec(memory_space=pltpu.SMEM),
-            pl.BlockSpec((rows_here, width), lambda i: (i, 0)),
-            pl.BlockSpec((width, 3 * mine * size), lambda i: (0, 0)),
+            pl.BlockSpec((rows_here, 3 * mine * size), lambda i: (i, 0)),
             pl.BlockSpec((mine, rows_here), lambda i: (0, i)),
             pl.BlockSpec((mine, size), lambda i: (0, 0)),
         ],
         out_specs=pl.BlockSpec((rows_here, mine * size), lambda i: (i, 0)),
         scratch_shapes=[pltpu.VMEM((mine, size, size), F32)],
-        compiler_params=pltpu.CompilerParams(vmem_limit_bytes=48 * 2**20),
-    )(lengths, everyone, weights, decays, gains)
+        compiler_params=pltpu.CompilerParams(vmem_limit_bytes=32 * 2**20),
+    )(lengths, qkv, decays, gains)
     back = lax.all_to_all(out, "seq", split_axis=0, concat_axis=1, tiled=True)
     return back.reshape(rows_here, heads_here, size)
 

time: 453 us -> 315 us (0.70)
  Pallas kernels: 48 us -> 230 us
  waiting for transfers between devices: 179 us -> 0 us
  blocking collectives: 170 us -> 79 us
  local copies, waits for them, and re-layouts: 33.1 us -> 6.15 us
  between operations: 13.4 us -> 0.06 us
  starting transfers between devices: 4.93 us -> 0 us
    pallas_call x1 -> x2, Pallas kernels: 48 us -> 230 us  [the longest x1 212 us: project_remote(): pl.pallas_call(functools.partial(gather_kernel, inner), out_shape=jax.Sha...]
    all_gather x2 -> x0, waiting for transfers between devices: 179 us -> none  [the longest x1 179 us: body(): gathered = lax.all_gather(half, 'seq', axis=0, tiled=True)]
    all_gather x1, blocking collectives: 124 us -> 32.6 us  [body(): decays = lax.all_gather(log_decay, 'seq', axis=1, tiled=True)]
    reshape x1 -> x0, local copies, waits for them, and re-layouts: 11.4 us -> none  [body(): weights = jnp.transpose(moved, (2, 0, 1, 3)).reshape(width, 3 * mine * size)]
    all_to_all x1 -> x0, local copies, waits for them, and re-layouts: 9.41 us -> none  [body(): lax.all_to_all(stacked, 'seq', split_axis=1, concat_axis=2, tiled=True)]
    all_to_all x1 -> x0, starting transfers between devices: 4.89 us -> none  [body(): lax.all_to_all(stacked, 'seq', split_axis=1, concat_axis=2, tiled=True)]
  transfers between devices with their start and end apart: 3 -> 0, of which waited for: 1 -> 0; matrix products, arithmetic and copies ran while one was open for 6% -> 0% of each run, Pallas kernels for 0% -> 0%
where the time goes in v2:
time: 315 us
  Pallas kernels  230 us (73%)
  blocking collectives  79 us (25%)
  local copies, waits for them, and re-layouts  6.15 us (2%)
    pallas_call x1, Pallas kernels, project_remote(): pl.pallas_call(functools.partial(gather_kernel, inner), out_shape=jax.Sha...  212 us
    all_to_all x1, blocking collectives, body(): back = lax.all_to_all(out, 'seq', split_axis=0, concat_axis=1, tiled=True)  46.4 us
    all_gather x1, blocking collectives, body(): decays = lax.all_gather(log_decay, 'seq', axis=1, tiled=True)  32.6 us
    pallas_call x1, Pallas kernels, body(): pl.pallas_call(functools.partial(attend_kernel, lengths.shape[0]), grid=(...  18 us

profile of v2, /device:TPU:0, one launch (start us, length us, event | category | flops | bytes accessed | tf_op | source)
XLA Modules:
  0.0 315.1 jit_solution(9907862522665481674)
XLA Ops:
  0.0 0.0 copy-start
  0.0 32.6 %all_gather.3 = bf16[16,4096]{1,0:T(8,128)(2,1)S(1)} all-gather(bf16[16,512]{1,0:T(8,128)(2,1)} %param.12), channel_id=1, replica_groups=mesh['groups'=2,'seq'=8,'head'=2] {'seq'}, dimensions={1}, use_global_device_ids=true | all-gather | bytes 147456 | tf_op jit(solution)/shard_map/all_gather | solution.py:332
  32.6 0.0 copy-done
  32.7 0.0 copy-start.2
  32.7 211.9 %shard_map.73.qkv_ref = bf16[4096,768]{1,0:T(8,128)(2,1)} custom-call(bf16[512,3072]{1,0:T(8,128)(2,1)} %tok_hbm.1, bf16[16,384,128]{2,1,0:T(8,128)(2,1)} %wq.1, bf16[16,384,128]{2,1,0:T(8,128)(2,1)} %wk.1, bf16[16,384,128]{2,1,0:T(8,128)(2,1)} %wv.1), custom_call_target="tpu_custom_call" | custom-call | tf_op jit(solution)/shard_map/pallas_call | solution.py:282
  244.6 0.0 copy-done.2
  244.6 0.0 copy-start.1
  244.6 2.8 copy-done.1
  247.4 18.0 %shard_map.74 = bf16[4096,256]{1,0:T(8,128)(2,1)S(1)} custom-call(s32[4]{0:T(128)S(1)} %copy-done.2, bf16[4096,768]{1,0:T(8,128)(2,1)S(1)} %copy-done.1, bf16[2,4096]{1,0:T(2,128)(2,1)S(1)} %constant_dynamic-slice_fusion.1.ld_ref, f32[2,128]{1,0:T(2,128)S(1)} %constant_dynamic-slice_fusion.gain_ref), custom_call_target="tpu_custom_call" | custom-call | tf_op jit(solution)/shard_map/pallas_call | solution.py:336
  265.4 46.4 %all_to_all.16 = bf16[8,512,256]{2,1,0:T(8,128)(2,1)S(1)} all-to-all(bf16[8,512,256]{2,1,0:T(8,128)(2,1)S(1)} %bitcast.2), channel_id=1, replica_groups=mesh['groups'=2,'seq'=8,'head'=2] {'seq'}, dimensions={0} | all-to-all | bytes 4194304 | tf_op jit(solution)/shard_map/all_to_all | solution.py:350
  311.8 1.2 copy.8
  313.0 2.1 reshape.7
  (2 shorter events, 0.0 us)
Async XLA Ops:
  0.0 32.6 %copy-start = (f32[16,128]{1,0:T(8,128)S(1)}, f32[16,128]{1,0:T(8,128)}, u32[]{:S(2)}) copy-start(f32[16,128]{1,0:T(8,128)} %param.11) | copy-start | bytes 24580
  32.7 211.9 %copy-start.2 = (s32[4]{0:T(128)S(1)}, s32[4]{0:T(128)}, u32[]{:S(2)}) copy-start(s32[4]{0:T(128)} %lens_ref.1) | copy-start | bytes 52
  244.6 2.8 copy-start.1

commit v3 on v2

--- a/solution.py
+++ b/solution.py
@@ -47,16 +47,7 @@
     return total
 
 
-def attend_kernel(prompts, lens_ref, qkv_ref, ld_ref, gain_ref, out_ref, state_ref):
-    step = pl.program_id(0)
-    heads = ld_ref.shape[0]
-    rows = qkv_ref.shape[0]
-    size = gain_ref.shape[1]
-
-    @pl.when(step == 0)
-    def _():
-        state_ref[...] = jnp.zeros_like(state_ref)
-
+def attend_shard(step, rows, heads, lens_ref, prompts, part, decay, gain, state_ref, store):
     ti = lax.broadcasted_iota(jnp.int32, (BLOCK, BLOCK), 0)
     si = lax.broadcasted_iota(jnp.int32, (BLOCK, BLOCK), 1)
     consts = ((ti >= si).astype(F32).astype(BF16), (ti < si).astype(F32).astype(BF16), ti < si)
@@ -73,19 +64,42 @@
             seg_t != seg_last,
             seg_before == seg_last,
         )
-        here = slice(b * BLOCK, (b + 1) * BLOCK)
         for h in range(heads):
-            part = [qkv_ref[here, (i * heads + h) * size : (i * heads + h + 1) * size] for i in range(3)]
             out, state = attend_block(
-                *part, ld_ref[h : h + 1, here], seg, state_ref[h], gain_ref[h : h + 1, :], consts
+                *part(b, h), decay(b, h), seg, state_ref[h], gain(h), consts
             )
             state_ref[h] = state
-            out_ref[here, h * size : (h + 1) * size] = out
+            store(b, h, out)
+
+
+def attend_kernel(prompts, lens_ref, qkv_ref, ld_ref, gain_ref, out_ref, state_ref):
+    step = pl.program_id(0)
+    heads = ld_ref.shape[0]
+    size = gain_ref.shape[1]
+
+    @pl.when(step == 0)
+    def _():
+        state_ref[...] = jnp.zeros_like(state_ref)
+
+    def here(b):
+        return slice(b * BLOCK, (b + 1) * BLOCK)
+
+    def part(b, h):
+        return [qkv_ref[here(b), (i * heads + h) * size : (i * heads + h + 1) * size] for i in range(3)]
+
+    def store(b, h, out):
+        out_ref[here(b), h * size : (h + 1) * size] = out
+
+    attend_shard(
+        step, qkv_ref.shape[0], heads, lens_ref, prompts, part,
+        lambda b, h: ld_ref[h : h + 1, here(b)], lambda h: gain_ref[h : h + 1, :], state_ref, store,
+    )
 
 
 def gather_kernel(
-    inner, tok_hbm, wq, wk, wv, out_ref, tok, landed, joined,
-    own_sem, w_own, z_send, y_send, core_send, tok_recv, w_send, w_recv,
+    inner, prompts, lens_ref, tok_hbm, wq, wk, wv, ld_ref, gain_ref, out_hbm,
+    tok, landed, joined, qkv, ready, decays, wide, state_ref,
+    own_sem, w_own, z_send, y_send, core_send, tok_recv, w_send, w_recv, d_send, d_recv, o_send, o_recv,
 ):
     count = lax.axis_size("seq")
     outer = count // inner
@@ -142,8 +156,30 @@
         s = (me + count - i) % count
         return remote(slot(m, s, half), slot(m, s, half), w_send.at[1, i, m], w_recv.at[half, s, m], twin)
 
+    def decay_copy(i):
+        src = decays.at[me]
+        return remote(src, src, d_send.at[i], d_recv.at[me], {"seq": (me + i) % count})
+
+    def decay_in(i):
+        s = (me + i) % count
+        return remote(decays.at[s], decays.at[s], d_send.at[i], d_recv.at[s], {"seq": s})
+
+    def columns_of(s):
+        return pl.ds(pl.multiple_of(s * (mine * size), 128), mine * size)
+
+    def result(s):
+        return remote(ready.at[s], out_hbm.at[:, columns_of(me)], o_send.at[s], o_recv.at[me], {"seq": s})
+
+    def result_in(i):
+        s = (me + i) % count
+        return remote(ready.at[s], out_hbm.at[:, columns_of(s)], o_send.at[s], o_recv.at[s], {"seq": s})
+
+    def own_result():
+        return pltpu.make_async_copy(ready.at[me], out_hbm.at[:, columns_of(me)], o_recv.at[me])
+
     for h in range(2):
         own_copy(h).start()
+    decays[me] = ld_ref[...]
     for m in range(3):
         own_weights(m).start()
     for h in range(2):
@@ -194,6 +230,8 @@
     for i in range(1, count):
         for m in range(3):
             weight_out(m, i).start()
+    for i in range(1, count):
+        decay_copy(i).start()
 
     last = 2 * outer - 1
 
@@ -213,8 +251,8 @@
         def _():
             crossing(j - 2, receive_and_start)
 
-        for k in range(2):
-            i = 2 * (j - 3) + 1 + k
+        for k in range(4):
+            i = 4 * (j - 3) + 1 + k
 
             @pl.when((i >= 1) & (i < count))
             def _():
@@ -224,7 +262,7 @@
 
         return carry
 
-    lax.fori_loop(1, last + 2, serve, 0)
+    lax.fori_loop(1, last, serve, 0)
 
     for m in range(3):
         own_weights(m).wait()
@@ -242,21 +280,72 @@
 
     lax.fori_loop(0, count, join, 0)
 
-    def project(i, carry):
-        s = (me + i) % count
-
-        @pl.when(i > 0)
-        def _():
-            arrived(s, 1 - core)
-
-        for h in range(2):
-            start = pl.multiple_of((2 * s + h) * rows, 16)
-            out_ref[pl.ds(start, rows), :] = jnp.dot(
-                tok[s, h], joined[...], preferred_element_type=F32
-            ).astype(BF16)
+    def project(j, carry):
+        step = (j + 1) // 2
+        place = far + jnp.where(j % 2 == 1, -step, step)
+
+        @pl.when((j >= last - 2) & (place >= 0) & (place < outer))
+        def _():
+            for k in range(1, inner):
+                s = place * inner + (near + k) % inner
+                receive_and_start(shard(s, core, core_send.at[k, j], other_core), s)
+
+        @pl.when((place >= 0) & (place < outer))
+        def _():
+            def one(k, carry):
+                s = place * inner + (near + k) % inner
+
+                @pl.when(s != me)
+                def _():
+                    arrived(s, 1 - core)
+
+                for h in range(2):
+                    start = pl.multiple_of((2 * s + h) * rows, 16)
+                    qkv[pl.ds(start, rows), :] = jnp.dot(
+                        tok[s, h], joined[...], preferred_element_type=F32
+                    ).astype(BF16)
+                return carry
+
+            lax.fori_loop(0, inner, one, 0)
+
         return carry
 
-    lax.fori_loop(0, count, project, 0)
+    lax.fori_loop(0, last, project, 0)
+
+    for i in range(1, count):
+        decay_in(i).wait_recv()
+    for b in range(wide.shape[1]):
+        wide[:, b] = decays[:, :, b * BLOCK : (b + 1) * BLOCK].astype(F32)
+    state_ref[...] = jnp.zeros_like(state_ref)
+    row_count = 2 * rows
+
+    def attend(s, carry):
+        def part(b, h):
+            here = pl.ds(pl.multiple_of(s * row_count + b * BLOCK, BLOCK), BLOCK)
+            return [qkv[here, (i * mine + h) * size : (i * mine + h + 1) * size] for i in range(3)]
+
+        def decay(b, h):
+            return wide[s, b, pl.ds(me * mine + h, 1), :].astype(BF16)
+
+        def store(b, h, out):
+            ready[s, b * BLOCK : (b + 1) * BLOCK, h * size : (h + 1) * size] = out
+
+        attend_shard(
+            s, row_count, mine, lens_ref, prompts, part, decay,
+            lambda h: gain_ref[pl.ds(me * mine + h, 1), :], state_ref, store,
+        )
+
+        @pl.when(s != me)
+        def _():
+            result(s).start()
+
+        @pl.when(s == me)
+        def _():
+            own_result().start()
+
+        return carry
+
+    lax.fori_loop(0, count, attend, 0)
 
     def drain(j, carry):
         forwards(j, lambda copy: copy.wait_send())
@@ -268,9 +357,15 @@
         for m in range(3):
             weight_out(m, i).wait_send()
             weight_over(m, i).wait_send()
-
-
-def project_remote(inner, tokens, w_query, w_key, w_value):
+    for i in range(1, count):
+        decay_copy(i).wait_send()
+    own_result().wait()
+    for i in range(1, count):
+        result((me + i) % count).wait_send()
+        result_in(i).wait_recv()
+
+
+def all_remote(inner, tokens, w_query, w_key, w_value, norm_gain, log_decay, lengths):
     rows_here, width = tokens.shape
     heads_here, depth, size = w_query.shape
     count = lax.axis_size("seq")
@@ -280,14 +375,21 @@
     anywhere = pl.BlockSpec(memory_space=pl.ANY)
     dma = pltpu.SemaphoreType.DMA
     return pl.pallas_call(
-        functools.partial(gather_kernel, inner),
-        out_shape=jax.ShapeDtypeStruct((rows_here * count, columns), BF16),
-        in_specs=[anywhere] * 4,
-        out_specs=pl.BlockSpec(memory_space=pltpu.VMEM),
+        functools.partial(gather_kernel, inner, lengths.shape[0]),
+        out_shape=jax.ShapeDtypeStruct((rows_here, heads_here * size), BF16),
+        in_specs=[pl.BlockSpec(memory_space=pltpu.SMEM)]
+        + [anywhere] * 4
+        + [pl.BlockSpec(memory_space=pltpu.VMEM)] * 2,
+        out_specs=anywhere,
         scratch_shapes=[
             pltpu.VMEM((count, 2, rows_here // 2, width), BF16),
             pltpu.VMEM((3, mine, width, size), BF16),
             pltpu.VMEM((width, columns), BF16),
+            pltpu.VMEM((rows_here * count, columns), BF16),
+            pltpu.VMEM((count, rows_here, mine * size), BF16),
+            pltpu.VMEM((count, heads_here, rows_here), BF16),
+            pltpu.VMEM((count, rows_here // BLOCK, heads_here, BLOCK), F32),
+            pltpu.VMEM((mine, size, size), F32),
             dma((2,)),
             dma((3,)),
             dma((2, 2 * outer)),
@@ -296,11 +398,15 @@
             dma((count, 2)),
             dma((2, count, 3)),
             dma((2, count, 3)),
+            dma((count,)),
+            dma((count,)),
+            dma((count,)),
+            dma((count,)),
         ],
         compiler_params=pltpu.CompilerParams(
             collective_id=0, has_side_effects=True, vmem_limit_bytes=56 * 2**20
         ),
-    )(tokens, w_query, w_key, w_value)
+    )(lengths, tokens, w_query, w_key, w_value, log_decay, norm_gain)
 
 
 def project_plain(tokens, w_query, w_key, w_value):
@@ -326,9 +432,9 @@
     fits = 2 * (total * width + total * 3 * mine * size + 6 * mine * size * width) < 48 * 2**20
     if fits and lax.axis_size("groups") % 2 == 0 and lax.axis_size("head") == 2:
         inner = 2 if count % 2 == 0 else 1
-        qkv = project_remote(inner, tokens, w_query, w_key, w_value)
-    else:
-        qkv = project_plain(tokens, w_query, w_key, w_value)
+        out = all_remote(inner, tokens, w_query, w_key, w_value, norm_gain, log_decay, lengths)
+        return out.reshape(rows_here, heads_here, size)
+    qkv = project_plain(tokens, w_query, w_key, w_value)
     decays = lax.all_gather(log_decay, "seq", axis=1, tiled=True)
     first_head = lax.axis_index("seq") * mine
     decays = lax.dynamic_slice_in_dim(decays, first_head, mine, axis=0)

time: 315 us -> 265 us (0.84)
  blocking collectives: 79 us -> 0 us
  Pallas kernels: 230 us -> 261 us
    all_to_all x1 -> x0, blocking collectives: 46.4 us -> none  [body(): back = lax.all_to_all(out, 'seq', split_axis=0, concat_axis=1, tiled=True)]
    all_gather x1 -> x0, blocking collectives: 32.6 us -> none  [body(): decays = lax.all_gather(log_decay, 'seq', axis=1, tiled=True)]
    pallas_call x2 -> x1, Pallas kernels: 230 us -> 261 us  [all_remote(): pl.pallas_call(functools.partial(gather_kernel, inner, lengths.shape[0]),...]
where the time goes in v3:
time: 265 us
  Pallas kernels  261 us (98%)
  local copies, waits for them, and re-layouts  3.54 us (1%)
    pallas_call x1, Pallas kernels, all_remote(): pl.pallas_call(functools.partial(gather_kernel, inner, lengths.shape[0]),...  261 us

profile of v3, /device:TPU:0, one launch (start us, length us, event | category | flops | bytes accessed | tf_op | source)
XLA Modules:
  0.0 265.0 jit_solution(2449896291510512760)
XLA Ops:
  0.0 261.4 %shard_map.73 = bf16[512,2048]{1,0:T(8,128)(2,1)} custom-call(s32[4]{0:T(128)} %lens_ref.1, bf16[512,3072]{1,0:T(8,128)(2,1)} %tok_hbm.1, bf16[16,384,128]{2,1,0:T(8,128)(2,1)} %wq.1, bf16[16,384,128]{2,1,0:T(8,128)(2,1)} %wk.1, bf16[16,384,128]{2,1,0:T(8,128)(2,1)} %wv.1, bf16[16,512]{1,0:T(8,128)(2,1)} %ld_ref.1, f32[16,128]{1,0:T(8,128)} %gain_ref.1), custom_call_target="tpu_custom_call" | custom-call | tf_op jit(solution)/shard_map/pallas_call | solution.py:377
  261.4 3.5 %copy.8 = bf16[64,8,16,128]{3,2,1,0:T(8,128)(2,1)} copy(bf16[64,8,16,128]{3,1,2,0:T(8,128)(2,1)} %bitcast.2) | data formatting | bytes 4194304

commit v4 on v3

--- a/solution.py
+++ b/solution.py
@@ -251,11 +251,9 @@
         def _():
             crossing(j - 2, receive_and_start)
 
-        for k in range(4):
-            i = 4 * (j - 3) + 1 + k
-
-            @pl.when((i >= 1) & (i < count))
-            def _():
+        @pl.when(j == 2)
+        def _():
+            for i in range(1, count):
                 for m in range(3):
                     weight_in(m, i, side).wait_recv()
                     weight_over(m, i).start()

time: 265 us -> 260 us (0.981)
  Pallas kernels: 261 us -> 256 us
    pallas_call x1, Pallas kernels: 261 us -> 256 us  [all_remote(): pl.pallas_call(functools.partial(gather_kernel, inner, lengths.shape[0]),...]
where the time goes in v4:
time: 260 us; the launch traced here: 259 us
  Pallas kernels  256 us (98%)
  local copies, waits for them, and re-layouts  3.54 us (1%)
    pallas_call x1, Pallas kernels, all_remote(): pl.pallas_call(functools.partial(gather_kernel, inner, lengths.shape[0]),...  256 us

profile of v4, /device:TPU:0, one launch (start us, length us, event | category | flops | bytes accessed | tf_op | source)
XLA Modules:
  0.0 259.4 jit_solution(9947890097027561242)
XLA Ops:
  0.0 255.9 %shard_map.73 = bf16[512,2048]{1,0:T(8,128)(2,1)} custom-call(s32[4]{0:T(128)} %lens_ref.1, bf16[512,3072]{1,0:T(8,128)(2,1)} %tok_hbm.1, bf16[16,384,128]{2,1,0:T(8,128)(2,1)} %wq.1, bf16[16,384,128]{2,1,0:T(8,128)(2,1)} %wk.1, bf16[16,384,128]{2,1,0:T(8,128)(2,1)} %wv.1, bf16[16,512]{1,0:T(8,128)(2,1)} %ld_ref.1, f32[16,128]{1,0:T(8,128)} %gain_ref.1), custom_call_target="tpu_custom_call" | custom-call | tf_op jit(solution)/shard_map/pallas_call | solution.py:375
  255.9 3.5 %copy.8 = bf16[64,8,16,128]{3,2,1,0:T(8,128)(2,1)} copy(bf16[64,8,16,128]{3,1,2,0:T(8,128)(2,1)} %bitcast.2) | data formatting | bytes 4194304
